TPU v7x, 256 devices: a whole 4x4x8 slice. The times are simulated.
256 devices in a mesh: row: 16 (over x_lo, z), col: 16 (over y, x_hi, core).
Axes of the slice: x: 4 (x_hi: 2, x_lo: 2; x = x_hi * 2 + x_lo), y: 4, z: 8, core: 2. Of those that a mesh axis runs over, the one named last changes fastest.
Arguments:
- features: bfloat16 [131072, 256], P(('row', 'col')), may hold values from -6 to 6
- tiles: int32 [16, 16, 96, 128, 128], P('row', 'col'), may hold values from 0 to 2
- tile_rows: int32 [16, 16, 96], P('row', 'col'), may hold values from 0 to 63
- tile_cols: int32 [16, 16, 96], P('row', 'col'), may hold values from 0 to 31, as said below
- tile_count: int32 [16, 16], P('row', 'col'), may hold values from 1 to 96, as said below
- panel_lists: int32 [16, 16, 16, 2], P('row', 'col'), may hold values from -1 to 3, as said below
- self_weight: bfloat16 [256, 256], replicated, may hold values from -0.375 to 0.375
- neigh_weight: bfloat16 [256, 256], replicated, may hold values from -6 to 6
- bias: float32 [256], replicated, may hold values from -3 to 3
Outputs:
- hidden: bfloat16 [131072, 256], P(('row', 'col'))
Inputs may be any that keep to these rules, and one draw needn't show every extreme that they name: `panel_lists`: every live tile names a non-empty list entry; each device reads exactly 2 distinct panels from at least one owner and 1 to 2 from every owner; empty entries come last in a list. `tile_cols`: every entry names a non-empty slot of the device's list. `tile_count`: some device holds 96 live tiles.
All inputs are finite; a program needn't handle non-finite values.
Results may differ from a plain program's by a relative error of at most 0.013.
Values may be sent and summed in bfloat16 or wider, within the bound.
A program may use at most 128 MiB of HBM per device.

v0:
```python
import jax
import jax.numpy as jnp
from jax import lax
from jax.sharding import PartitionSpec as P


def shards(
    features, tiles, tile_rows, tile_cols, tile_count, panel_lists, self_weight, neigh_weight, bias
):
    tile_size = tiles.shape[-1]
    feat_width = features.shape[1]
    panels = features.shape[0] // tile_size
    capacity = panel_lists.shape[-1]
    wanted_lists = panel_lists[0, 0]
    entries = tile_cols[0, 0]
    owners = entries // capacity
    slot_index = entries % capacity
    local_panels = features.reshape(panels, tile_size, feat_width)
    column_block = lax.all_gather(local_panels, "row", axis=0, tiled=True)
    chosen = wanted_lists[owners, slot_index]
    panel_index = owners * panels + jnp.maximum(chosen, 0)
    operand = column_block[panel_index]
    live_tiles = jnp.arange(tiles.shape[2], dtype=jnp.int32) < tile_count[0, 0]
    masked = jnp.where(live_tiles[:, None, None], tiles[0, 0], 0)
    blocks = masked.astype(jnp.bfloat16)
    products = jnp.einsum("tab,tbf->taf", blocks, operand, preferred_element_type=jnp.float32)
    row_panels = panels * lax.axis_size("col")
    row_index = tile_rows[0, 0]
    partial_value = (
        jnp.zeros((row_panels, tile_size, feat_width), jnp.float32).at[row_index].add(products)
    )
    counts = (
        jnp.zeros((row_panels, tile_size), jnp.float32)
        .at[row_index]
        .add(jnp.sum(masked, axis=2).astype(jnp.float32))
    )
    rounded = partial_value.reshape(row_panels * tile_size, feat_width).astype(jnp.bfloat16)
    summed = lax.psum_scatter(rounded, "col", scatter_dimension=0, tiled=True).astype(jnp.float32)
    degree = lax.psum_scatter(
        counts.reshape(row_panels * tile_size).astype(jnp.bfloat16),
        "col",
        scatter_dimension=0,
        tiled=True,
    ).astype(jnp.float32)
    mean_rows = (summed / jnp.maximum(degree, 1.0)[:, None]).astype(jnp.bfloat16)
    joined = jnp.concatenate([features, mean_rows], axis=1)
    stacked_weight = jnp.concatenate([self_weight, neigh_weight], axis=0)
    mixed = jnp.dot(joined, stacked_weight, preferred_element_type=jnp.float32) + bias
    return jnp.maximum(mixed, 0.0).astype(jnp.bfloat16)


def solution(mesh):
    return jax.shard_map(
        shards,
        mesh=mesh,
        in_specs=(
            P(("row", "col"), None),
            P("row", "col", None, None, None),
            P("row", "col", None),
            P("row", "col", None),
            P("row", "col"),
            P("row", "col", None, None),
            P(),
            P(),
            P(),
        ),
        out_specs=P(("row", "col"), None),
        check_vma=False,
    )
```

profile of v0, /device:TPU:24, one launch (start us, length us, event | category | flops | bytes accessed | tf_op | source)
XLA Modules:
  0.0 241.1 jit_solution(10756746933126380848)
XLA Ops:
  6.5 0.0 copy-start
  6.5 0.0 all-gather.2.cloned.1.call-start
  6.5 0.7 all-gather.2.cloned.1.call-update
  7.3 0.0 reduce-scatter.2.cloned.1.call-start
  8.0 0.7 fusion.24
  8.6 0.0 copy-done
  8.6 1.5 gather_fusion
  10.2 0.7 fusion.17
  10.8 77.9 %all-gather.2.cloned.1.call-done = bf16[64,128,256]{2,1,0:T(8,128)(2,1)} async-done(((bf16[4,128,256]{2,1,0:T(8,128)(2,1)}), bf16[64,128,256]{2,1,0:T(8,128)(2,1)}) %all-gather.2.cloned.1.call-update) | async-done | bytes 4194320 | tf_op jit(solution)/shard_map/all_gather | solution.py:19
  88.7 8.1 %gather_fusion.1 = bf16[96,128,256]{2,1,0:T(8,128)(2,1)} fusion(bf16[64,128,256]{2,1,0:T(8,128)(2,1)} %all-gather.2.cloned.1.call-done, s32[1024]{0:T(1024)S(1)} %pad_clamp_fusion), kind=kCustom, calls=%fused_computation.1 | custom fusion | bytes 12583296 | tf_op jit(solution)/shard_map/gather | solution.py:22
  96.9 11.0 %fusion.2 = f32[96,128,256]{2,1,0:T(8,128)} fusion(bf16[96,128,256]{2,1,0:T(8,128)(2,1)} %gather_fusion.1, s32[1,1,96,128,128]{4,3,2,1,0:T(8,128)} %param.10, pred[96]{0:T(512)(128)(4,1)S(1)} %iota_compare_fusion), kind=kOutput, calls=%fused_computation.7 | convolution fusion | flops 808452096 | bytes 25165920 | tf_op jit(solution)/shard_map/tab,tbf->taf/dot_general | solution.py:26
  107.9 4.2 %broadcast_in_dim.16 = f32[64,128,256]{2,1,0:T(8,128)} broadcast(f32[]{:T(128)} %constant.32.clone.1), dimensions={} | broadcast | bytes 8388612 | tf_op jit(solution)/shard_map/broadcast_in_dim | solution.py:30
  112.1 28.7 %scatter_fusion = f32[64,128,256]{2,1,0:T(8,128)} fusion(f32[64,128,256]{2,1,0:T(8,128)} %broadcast_in_dim.16, s32[96]{0:T(128)S(1)} %fusion.17, f32[96,128,256]{2,1,0:T(8,128)} %fusion.2), kind=kCustom, calls=%fused_computation.2 | custom fusion | flops 3145728 | bytes 37749120 | tf_op jit(solution)/shard_map/scatter-add | solution.py:30
  140.8 5.9 %convert_element_type.31 = bf16[64,128,256]{2,1,0:T(8,128)(2,1)} convert(f32[64,128,256]{2,1,0:T(8,128)} %scatter_fusion) | non-fusion elementwise | flops 2097152 | bytes 12582912 | tf_op jit(solution)/shard_map/convert_element_type | solution.py:37
  146.7 0.0 copy-start.4
  146.8 0.0 reduce-scatter.2.cloned.1.call-update
  146.8 4.6 %fusion = s32[96,128]{1,0:T(8,128)S(1)} fusion(s32[1,1,96,128,128]{4,3,2,1,0:T(8,128)} %param.10, pred[96]{0:T(512)(128)(4,1)S(1)} %iota_compare_fusion), kind=kLoop, calls=%fused_computation.5 | loop fusion | flops 3133440 | bytes 6340704 | tf_op jit(solution)/shard_map/reduce_sum | solution.py:35
  151.4 0.9 scatter_custom_fusion.1
  152.4 0.6 dynamic-slice
  153.6 55.6 %all-reduce = bf16[8192]{0:T(1024)(128)(2,1)S(1)} all-reduce(bf16[8192]{0:T(1024)(128)(2,1)S(1)} %convert_bitcast_fusion), channel_id=3, replica_groups=mesh['row'=16,'col'=16] {'col'}, use_global_device_ids=true, to_apply=%region_4.5.clone | all-reduce | flops 8192 | bytes 32768
  209.2 0.1 convert_maximum_fusion
  209.3 22.8 %reduce-scatter.2.cloned.1.call-done = bf16[512,256]{1,0:T(8,128)(2,1)} async-done(((bf16[8192,256]{1,0:T(8,128)(2,1)}), bf16[512,256]{1,0:T(8,128)(2,1)}) %reduce-scatter.2.cloned.1.call-update) | async-done | bytes 262160 | tf_op jit(solution)/shard_map/reduce_scatter | solution.py:38
  232.1 1.1 divide_convert_fusion
  233.2 1.0 fusion.7
  (13 shorter events, 0.0 us)
Async XLA Ops:
  6.5 2.1 copy-start
  6.5 82.2 %all-gather.2.cloned.1.call-start = ((), (), s32[]{:S(2)}) async-start(), calls=%async_computation.1 | async-start | bytes 4456448 | tf_op jit(solution)/shard_map/all_gather | solution.py:19
  7.3 224.9 %reduce-scatter.2.cloned.1.call-start = ((), (), s32[]{:S(2)}) async-start(), calls=%async_computation.2 | async-start | bytes 4456448 | tf_op jit(solution)/shard_map/reduce_scatter | solution.py:38
  146.7 5.7 %copy-start.5 = (u32[256]{0:T(256)S(1)}, u32[256]{0:T(256)}, u32[]{:S(2)}) copy-start(u32[256]{0:T(256)} %constant.61) | copy-start | bytes 3076
  146.7 86.5 %copy-start.1 = (bf16[512,256]{1,0:T(8,128)(2,1)S(1)}, bf16[512,256]{1,0:T(8,128)(2,1)}, u32[]{:S(2)}) copy-start(bf16[512,256]{1,0:T(8,128)(2,1)} %param.9) | copy-start | bytes 786436
  146.7 86.5 %copy-start.2 = (bf16[256,256]{1,0:T(8,128)(2,1)S(1)}, bf16[256,256]{1,0:T(8,128)(2,1)}, u32[]{:S(2)}) copy-start(bf16[256,256]{1,0:T(8,128)(2,1)} %param.16) | copy-start | bytes 393220
  146.7 86.5 %copy-start.3 = (bf16[256,256]{1,0:T(8,128)(2,1)S(1)}, bf16[256,256]{1,0:T(8,128)(2,1)}, u32[]{:S(2)}) copy-start(bf16[256,256]{1,0:T(8,128)(2,1)} %param.15) | copy-start | bytes 393220
  146.7 86.5 %copy-start.4 = (f32[256]{0:T(256)S(1)}, f32[256]{0:T(256)}, u32[]{:S(2)}) copy-start(f32[256]{0:T(256)} %param.17) | copy-start | bytes 3076
Sparse Core Ops, SparseCore 0:
  9.1 79.5 all-gather.1
  146.9 85.1 reduce-scatter.1
where the time goes:
time: 242 us; the launch traced here: 241 us
  waiting for transfers between devices  101 us (42%)
  blocking collectives  55.6 us (23%)
  other arithmetic  42.7 us (18%)
  between operations  14.8 us (6%)
  local copies, waits for them, and re-layouts  14.5 us (6%)
  matrix products  12 us (5%)
    all_gather x1, waiting for transfers between devices, shards(): column_block = lax.all_gather(local_panels, 'row', axis=0, tiled=True)  77.9 us
    unnamed x1, blocking collectives  55.6 us
    scatter-add x1, other arithmetic, shards(): jnp.zeros((row_panels, tile_size, feat_width), jnp.float32).at[row_index]  28.7 us
    reduce_scatter x1, waiting for transfers between devices, shards(): lax.psum_scatter(rounded, 'col', scatter_dimension=0, tiled=True)  22.8 us
    dot_general x1, matrix products, shards(): jnp.einsum('tab,tbf->taf', blocks, operand, preferred_element_type=jnp.fl...  11 us
    gather x1, local copies, waits for them, and re-layouts, shards(): operand = column_block[panel_index]  8.14 us
    convert_element_type x1, other arithmetic, shards(): partial_value.reshape(row_panels * tile_size, feat_width)  5.92 us
  transfers between devices with their start and end apart: 2, of which 2 were waited for; matrix products, arithmetic and copies ran while one was open for 4% of the time, Pallas kernels for 0%

commit v1 on v0

v1 whole, which is shorter than its diff:
```python
import functools

import jax
import jax.numpy as jnp
from jax import lax
from jax.experimental import pallas as pl
from jax.experimental.pallas import tpu as pltpu
from jax.sharding import PartitionSpec as P

MESH = pl.DeviceIdType.MESH
Z = 8
Y = 4
TILE = 128
HALVES = 2
PANELS = 4
TILES = 96
CAP = 2
COLS = 16
ROWS = 16
CHUNKS = 4
YFIRST = (4, 2)

F32 = jnp.float32
BF16 = jnp.bfloat16


class Sems:
    def __init__(self, send, recv):
        self.send, self.recv, self.used, self.copies = send, recv, 0, []

    def copy(self, src, dst, device):
        n = self.used
        self.used += 1
        c = pltpu.make_async_remote_copy(
            src_ref=src,
            dst_ref=dst,
            send_sem=self.send.at[n],
            recv_sem=self.recv.at[n],
            device_id=device,
            device_id_type=MESH,
        )
        self.copies.append(c)
        return c


def kernel(
    feat_ref,
    tiles_ref,
    rows_ref,
    cols_ref,
    count_ref,
    lists_ref,
    lists_vec_ref,
    ws_ref,
    wn_ref,
    bias_ref,
    out_ref,
    *scratch,
):
    s = dict(zip(SCRATCH_NAMES, scratch))
    r, c = lax.axis_index("row"), lax.axis_index("col")
    x_lo, z = r // Z, lax.rem(r, Z)
    y, x_hi, core = c // 4, lax.rem(c // 2, 2), lax.rem(c, 2)

    def z_at(d):
        return lax.rem(z + d + Z, Z)

    def at_z(d):
        return (x_lo * Z + z_at(d), c)

    def at_y(d):
        return (r, lax.rem(c + 4 * d, COLS))

    x_pair = ((1 - x_lo) * Z + z, c)
    x_far = (r, c + 2 - 4 * x_hi)
    sibling = (r, c + 1 - 2 * core)

    local = s["local_sem"]
    own_copies = []
    for h in range(HALVES):
        cp = pltpu.make_async_copy(
            feat_ref.at[:, :, pl.ds(h * TILE, TILE)], s["own"].at[h], local.at[h]
        )
        cp.start()
        own_copies.append(cp)
    per = TILES // CHUNKS
    tile_copies = []
    for k in range(CHUNKS):
        part = pl.ds(k * per, per)
        cp = pltpu.make_async_copy(
            tiles_ref.at[part], s["tiles32"].at[part], local.at[HALVES + k]
        )
        cp.start()
        tile_copies.append(cp)
    s["lists_out"][...] = jnp.zeros((8, TILE), jnp.int32)
    s["lists_out"][0:1, 0 : ROWS * CAP] = lists_vec_ref[...]

    barrier = pltpu.get_barrier_semaphore()
    peers = [at_z(1), at_z(-1), x_pair]
    for k in range(1, COLS):
        peers.append((r, lax.rem(c + k, COLS)))
    for peer in peers:
        pl.semaphore_signal(barrier, inc=1, device_id=peer, device_id_type=MESH)
    pl.semaphore_wait(barrier, len(peers))

    sems = Sems(s["send_sem"], s["recv_sem"])
    for cp in own_copies:
        cp.wait()

    fwd = [[s[f"fwd{h}{k}"] for k in range(3)] for h in range(HALVES)]
    bwd = [[s[f"bwd{h}{k}"] for k in range(3)] for h in range(HALVES)]
    opp = [s["opp0"], s["opp1"]]
    oper = [s["oper0"], s["oper1"]]
    ring = {}
    for h in range(HALVES):
        for k in range(4):
            if k < 3:
                src_f = s["own"].at[h] if k == 0 else fwd[h][k - 1]
                src_b = s["own"].at[h] if k == 0 else bwd[h][k - 1]
                dst_f, dst_b = fwd[h][k], bwd[h][k]
            else:
                src_f, dst_f = fwd[h][2].at[pl.ds(0, 2)], opp[h].at[pl.ds(0, 2)]
                src_b, dst_b = bwd[h][2].at[pl.ds(2, 2)], opp[h].at[pl.ds(2, 2)]
            ring[h, 0, k] = sems.copy(src_f, dst_f, at_z(1))
            ring[h, 1, k] = sems.copy(src_b, dst_b, at_z(-1))
    lists_copy = sems.copy(s["lists_out"], s["lists_in"], x_pair)

    for h in range(HALVES):
        ring[h, 0, 0].start()
        ring[h, 1, 0].start()
    lists_copy.start()

    pair_copies = {}

    def select(h, slot, block, dist):
        owner = x_lo * Z + z_at(dist)
        for j in range(CAP):
            mine = jnp.maximum(lists_ref[0, owner * CAP + j], 0)
            oper[h][owner * CAP + j] = block[mine]
        for j in range(CAP):
            theirs = jnp.maximum(s["lists_smem"][0, owner * CAP + j], 0)
            s[f"pair{h}"][slot * CAP + j] = block[theirs]
        cp = sems.copy(
            s[f"pair{h}"].at[pl.ds(slot * CAP, CAP)],
            oper[h].at[pl.ds(owner * CAP, CAP)],
            x_pair,
        )
        cp.start()
        pair_copies[h, slot] = cp

    live = count_ref[0, 0]
    lane = lax.broadcasted_iota(jnp.int32, (TILE, TILE), 1)
    sub = lax.broadcasted_iota(jnp.int32, (TILE, TILE), 0)
    s["rows"][...] = jnp.full((8, TILE), -1, jnp.int32)
    s["rows"][0:1, 0:TILES] = rows_ref[...]
    row_l = jnp.broadcast_to(s["rows"][0:1, :], (TILE, TILE))
    row_l = jnp.where(lane < live, row_l, -1)
    row_s = jnp.transpose(row_l.astype(F32)).astype(jnp.int32)
    prev = jnp.max(jnp.where((row_s == row_l) & (sub < lane), sub, -1), axis=0, keepdims=True)
    prev = jnp.where(prev < 0, TILES, prev)
    last = jnp.max(jnp.where(row_s == lane, sub, -1), axis=0, keepdims=True)
    last = jnp.where(last < 0, TILES, last)
    s["meta"][0:1, :] = prev
    s["meta"][1:2, :] = last
    s["meta"][2:8, :] = jnp.zeros((6, TILE), jnp.int32)
    meta_copy = pltpu.make_async_copy(s["meta"], s["meta_smem"], local.at[HALVES + CHUNKS])
    meta_copy.start()

    for h in range(HALVES):
        s[f"sums{h}"][TILES] = jnp.zeros((TILE, TILE), F32)

    lists_copy.wait_recv()
    smem_copy = pltpu.make_async_copy(
        s["lists_in"], s["lists_smem"], local.at[HALVES + CHUNKS + 1]
    )
    smem_copy.start()
    smem_copy.wait()
    for h in range(HALVES):
        select(h, 0, s["own"].at[h], 0)

    ones = jnp.ones((16, TILE), BF16)

    def prepare(k):
        tile_copies[k].wait()

        def body(t, _):
            block = s["tiles32"][t].astype(F32).astype(BF16)
            s["blocks"][t] = block
            sums = lax.dot_general(
                ones, block, (((1,), (1,)), ((), ())), preferred_element_type=F32
            )
            s["degs"][pl.ds(t, 1), :] = sums[0:1, :]
            return 0

        lax.fori_loop(k * per, (k + 1) * per, body, 0, unroll=4)

    def arrive(h, k):
        for way in (0, 1):
            ring[h, way, k].wait_recv()
            if k < 3:
                ring[h, way, k + 1].start()
        if k < 3:
            select(h, 1 + k, fwd[h][k], -(k + 1))
            select(h, 4 + k, bwd[h][k], k + 1)
        else:
            select(h, 7, opp[h], 4)

    def base(i):
        mixed = jnp.dot(s["own"][0, i], ws_ref[0:TILE, :], preferred_element_type=F32)
        mixed += jnp.dot(s["own"][1, i], ws_ref[TILE : 2 * TILE, :], preferred_element_type=F32)
        s["mixed"][i] = mixed + bias_ref[...]

    for k in range(4):
        prepare(k)
        for h in range(HALVES):
            arrive(h, k)
        base(k)

    q = lax.broadcasted_iota(jnp.int32, (TILE, TILE), 0)
    panel = jnp.where(lax.rem(q, 8) < 4, (q // 8) * 4 + lax.rem(q, 8), -2)
    hot = (panel == row_l).astype(F32).astype(BF16)
    s["degs"][TILES:TILE, :] = jnp.zeros((TILE - TILES, TILE), F32)
    degs = jnp.dot(hot, s["degs"][...].astype(BF16), preferred_element_type=F32)
    s["deg_out"][...] = degs.reshape(COLS, 8, TILE)
    deg_copies = []
    for k in range(1, COLS):
        to = lax.rem(c + k, COLS)
        cp = sems.copy(s["deg_out"].at[to], s["deg_in"].at[k - 1], (r, to))
        cp.start()
        deg_copies.append(cp)

    meta_copy.wait()

    def products(h):
        for slot in range(8):
            pair_copies[h, slot].wait_recv()
        sums = s[f"sums{h}"]

        def body(t, _):
            value = jnp.dot(
                s["blocks"][t], oper[h][cols_ref[0, t]], preferred_element_type=F32
            )
            sums[t] = value + sums[s["meta_smem"][0, t]]
            return 0

        lax.fori_loop(0, TILES, body, 0, unroll=4)

    def owner_col(dy, dx, which):
        hi = x_hi if dx == 0 else 1 - x_hi
        return lax.rem(y + dy, Y) * 4 + hi * 2 + which

    order = [(2, 1), (2, 0), (1, 1), (1, 0), (3, 1), (3, 0), (0, 1), (0, 0)]
    swap = {}

    def partial(h, dy, dx, which, i):
        p = owner_col(dy, dx, which) * PANELS + i
        return s[f"sums{h}"][s["meta_smem"][1, p]]

    def exchange(h):
        for dy, dx in order:
            j = dy * 2 + dx

            def body(i, _):
                s["swap_out"][h, j * PANELS + i] = partial(h, dy, dx, 1 - core, i).astype(BF16)
                return 0

            lax.fori_loop(0, PANELS, body, 0, unroll=True)
            part = pl.ds(j * PANELS, PANELS)
            cp = sems.copy(s["swap_out"].at[h, part], s["swap_in"].at[h, part], sibling)
            cp.start()
            swap[h, j] = cp

    def both(h, dy, dx, i):
        j = dy * 2 + dx
        return partial(h, dy, dx, core, i) + s["swap_in"][h, j * PANELS + i].astype(F32)

    stage1, stage2 = {}, {}

    def first(h):
        n = YFIRST[h]
        m = PANELS - n
        arrived = set()

        def need(dy, dx):
            if (dy, dx) not in arrived:
                arrived.add((dy, dx))
                swap[h, dy * 2 + dx].wait_recv()

        for dy in (2, 1, 3):
            need(dy, 1)
            need(dy, 0)
            if n:
                for dx in (1, 0):
                    for i in range(n):
                        s[f"y1_out{h}"][dy - 1, dx * n + i] = both(h, dy, dx, i).astype(BF16)
                cp = sems.copy(
                    s[f"y1_out{h}"].at[dy - 1], s[f"y1_in{h}"].at[dy - 1], at_y(dy)
                )
                cp.start()
                stage1[h, dy] = cp
            if m:
                for i in range(m):
                    s[f"x1_out{h}"][dy, i] = both(h, dy, 1, n + i).astype(BF16)
                cp = sems.copy(s[f"x1_out{h}"].at[dy], s[f"x1_in{h}"].at[dy], x_far)
                cp.start()
                stage1[h, "x", dy] = cp
        need(0, 1)
        need(0, 0)
        if m:
            for i in range(m):
                s[f"x1_out{h}"][0, i] = both(h, 0, 1, n + i).astype(BF16)
            cp = sems.copy(s[f"x1_out{h}"].at[0], s[f"x1_in{h}"].at[0], x_far)
            cp.start()
            stage1[h, "x", 0] = cp

    def second(h):
        n = YFIRST[h]
        m = PANELS - n
        if m:
            for dy in (2, 1, 3):
                stage1[h, "x", dy].wait_recv()
                for i in range(m):
                    total = both(h, dy, 0, n + i) + s[f"x1_in{h}"][dy, i].astype(F32)
                    s[f"y2_out{h}"][dy - 1, i] = total.astype(BF16)
                cp = sems.copy(
                    s[f"y2_out{h}"].at[dy - 1], s[f"y2_in{h}"].at[dy - 1], at_y(dy)
                )
                cp.start()
                stage2[h, dy] = cp
        if n:
            for dy in (2, 1, 3):
                stage1[h, dy].wait_recv()
            for i in range(n):
                total = both(h, 0, 1, i)
                for dy in (2, 1, 3):
                    total += s[f"y1_in{h}"][dy - 1, n + i].astype(F32)
                s[f"x2_out{h}"][i] = total.astype(BF16)
            cp = sems.copy(s[f"x2_out{h}"], s[f"x2_in{h}"], x_far)
            cp.start()
            stage2[h, "x"] = cp

    def third(h):
        n = YFIRST[h]
        m = PANELS - n
        if m:
            stage1[h, "x", 0].wait_recv()
            for dy in (2, 1, 3):
                stage2[h, dy].wait_recv()
        if n:
            stage2[h, "x"].wait_recv()
        for i in range(PANELS):
            total = both(h, 0, 0, i)
            if i < n:
                for dy in (2, 1, 3):
                    total += s[f"y1_in{h}"][dy - 1, i].astype(F32)
                total += s[f"x2_in{h}"][i].astype(F32)
            else:
                total += s[f"x1_in{h}"][0, i - n].astype(F32)
                for dy in (2, 1, 3):
                    total += s[f"y2_in{h}"][dy - 1, i - n].astype(F32)
            mean = (total / s["deg"][i]).astype(BF16)
            s["mixed"][i] += jnp.dot(
                mean, wn_ref[h * TILE : (h + 1) * TILE, :], preferred_element_type=F32
            )

    def degree():
        total = s["deg_out"][c]
        for k in range(1, COLS):
            deg_copies[k - 1].wait_recv()
            total += s["deg_in"][k - 1]
        total = jnp.maximum(total, 1.0)
        wide = jnp.transpose(jnp.concatenate([total] * 16, axis=0))
        for i in range(PANELS):
            s["deg"][i] = jnp.broadcast_to(wide[:, i : i + 1], (TILE, TILE))

    products(0)
    exchange(0)
    degree()
    first(0)
    products(1)
    exchange(1)
    first(1)
    second(0)
    second(1)
    third(0)
    third(1)
    for i in range(PANELS):
        out_ref[pl.ds(i * TILE, TILE), :] = jnp.maximum(s["mixed"][i], 0.0).astype(BF16)
    for cp in sems.copies:
        cp.wait_send()


def scratch_spec():
    panel = lambda *lead: pltpu.VMEM((*lead, TILE, TILE), BF16)
    spec = {
        "send_sem": pltpu.SemaphoreType.DMA((96,)),
        "recv_sem": pltpu.SemaphoreType.DMA((96,)),
        "local_sem": pltpu.SemaphoreType.DMA((HALVES + CHUNKS + 2,)),
        "own": panel(HALVES, PANELS),
        "tiles32": pltpu.VMEM((TILES, TILE, TILE), jnp.int32),
        "blocks": panel(TILES),
        "degs": pltpu.VMEM((TILE, TILE), F32),
        "deg_out": pltpu.VMEM((COLS, 8, TILE), F32),
        "deg_in": pltpu.VMEM((COLS - 1, 8, TILE), F32),
        "deg": pltpu.VMEM((PANELS, TILE, TILE), F32),
        "rows": pltpu.VMEM((8, TILE), jnp.int32),
        "meta": pltpu.VMEM((8, TILE), jnp.int32),
        "meta_smem": pltpu.SMEM((8, TILE), jnp.int32),
        "lists_out": pltpu.VMEM((8, TILE), jnp.int32),
        "lists_in": pltpu.VMEM((8, TILE), jnp.int32),
        "lists_smem": pltpu.SMEM((8, TILE), jnp.int32),
        "mixed": pltpu.VMEM((PANELS, TILE, 2 * TILE), F32),
        "swap_out": panel(HALVES, 8 * PANELS),
        "swap_in": panel(HALVES, 8 * PANELS),
    }
    for h in range(HALVES):
        for k in range(3):
            spec[f"fwd{h}{k}"] = panel(PANELS)
            spec[f"bwd{h}{k}"] = panel(PANELS)
        spec[f"opp{h}"] = panel(PANELS)
        spec[f"oper{h}"] = panel(ROWS * CAP)
        spec[f"pair{h}"] = panel(8 * CAP)
        spec[f"sums{h}"] = pltpu.VMEM((TILES + 1, TILE, TILE), F32)
        n = YFIRST[h]
        m = PANELS - n
        if n:
            spec[f"y1_out{h}"] = panel(3, 2 * n)
            spec[f"y1_in{h}"] = panel(3, 2 * n)
            spec[f"x2_out{h}"] = panel(n)
            spec[f"x2_in{h}"] = panel(n)
        if m:
            spec[f"x1_out{h}"] = panel(4, m)
            spec[f"x1_in{h}"] = panel(4, m)
            spec[f"y2_out{h}"] = panel(3, m)
            spec[f"y2_in{h}"] = panel(3, m)
    return spec


SCRATCH_NAMES = list(scratch_spec())


def shards(
    features, tiles, tile_rows, tile_cols, tile_count, panel_lists, self_weight, neigh_weight, bias
):
    vmem = pl.BlockSpec(memory_space=pltpu.VMEM)
    smem = pl.BlockSpec(memory_space=pltpu.SMEM)
    hbm = pl.BlockSpec(memory_space=pl.ANY)
    lists = panel_lists.reshape(1, ROWS * CAP)
    return pl.pallas_call(
        kernel,
        out_shape=jax.ShapeDtypeStruct((PANELS * TILE, 2 * TILE), BF16),
        in_specs=[hbm, hbm, vmem, smem, smem, smem, vmem, vmem, vmem, vmem],
        out_specs=vmem,
        scratch_shapes=list(scratch_spec().values()),
        compiler_params=pltpu.CompilerParams(
            collective_id=0, has_side_effects=True, vmem_limit_bytes=56 << 20
        ),
        name="sage",
    )(
        features.reshape(PANELS, TILE, 2 * TILE),
        tiles[0, 0],
        tile_rows[0],
        tile_cols[0],
        tile_count,
        lists,
        lists,
        self_weight,
        neigh_weight,
        bias.reshape(1, 2 * TILE),
    )


def solution(mesh):
    return jax.shard_map(
        shards,
        mesh=mesh,
        in_specs=(
            P(("row", "col"), None),
            P("row", "col", None, None, None),
            P("row", "col", None),
            P("row", "col", None),
            P("row", "col"),
            P("row", "col", None, None),
            P(),
            P(),
            P(),
        ),
        out_specs=P(("row", "col"), None),
        check_vma=False,
    )
```

time: 242 us -> 73.9 us (0.31)
  the two profiles are of different devices: /device:TPU:24 before, /device:TPU:1 now
where the time goes in v1:
time: 73.9 us; the launch traced here: 73.8 us
  Pallas kernels  70.1 us (95%)
  local copies, waits for them, and re-layouts  3.03 us (4%)
    pallas_call x1, Pallas kernels, shards(): pl.pallas_call(kernel, out_shape=jax.ShapeDtypeStruct((PANELS * TILE, 2 *...  70.1 us
    unnamed x2, local copies, waits for them, and re-layouts  2.43 us

profile of v1, /device:TPU:1, one launch (start us, length us, event | category | flops | bytes accessed | tf_op | source)
XLA Modules:
  0.0 73.8 jit_solution(14381404522015503336)
XLA Ops:
  0.7 0.8 %copy.11 = s32[1,1,16,2]{3,2,1,0:T(8,128)S(1)} copy(s32[1,1,16,2]{2,3,1,0:T(2,128)} %param.14) | data formatting | bytes 256 | tf_op args[5]
  1.4 0.6 reshape.10.lists_ref.lists_vec_ref
  2.0 70.1 %sage.1 = bf16[512,256]{1,0:T(8,128)(2,1)} custom-call(bf16[4,128,256]{2,1,0:T(8,128)(2,1)} %bitcast.8, s32[96,128,128]{2,1,0:T(8,128)} %bitcast.7, s32[1,96]{1,0:T(1,128)} %bitcast.10, s32[1,96]{1,0:T(1,128)} %bitcast.11, s32[1,1]{1,0:T(1,128)S(6)} %copy.13.count_ref, s32[1,32]{1,0:T(1,128)} %reshape.10.lists_ref.lists_vec_ref, ...), custom_call_target="tpu_custom_call" | custom-call | tf_op jit(solution)/shard_map/sage/pallas_call | solution.py:449
  72.1 1.7 %copy.14 = bf16[512,256]{1,0:T(8,128)(2,1)} copy(bf16[512,256]{1,0:T(8,128)(2,1)} %sage.1) | data formatting | bytes 524288

commit v2 on v1

--- a/solution.py
+++ b/solution.py
@@ -18,7 +18,7 @@
 COLS = 16
 ROWS = 16
 CHUNKS = 4
-YFIRST = (4, 2)
+YFIRST = (2, 2)
 
 F32 = jnp.float32
 BF16 = jnp.bfloat16
@@ -92,13 +92,16 @@
         )
         cp.start()
         tile_copies.append(cp)
+    weight_copies = []
+    for k, (src, dst) in enumerate(((ws_ref, s["ws"]), (wn_ref, s["wn"]))):
+        cp = pltpu.make_async_copy(src, dst, local.at[HALVES + CHUNKS + 2 + k])
+        cp.start()
+        weight_copies.append(cp)
     s["lists_out"][...] = jnp.zeros((8, TILE), jnp.int32)
-    s["lists_out"][0:1, 0 : ROWS * CAP] = lists_vec_ref[...]
+    s["lists_out"][0:CAP, 0:ROWS] = lists_vec_ref[...]
 
     barrier = pltpu.get_barrier_semaphore()
-    peers = [at_z(1), at_z(-1), x_pair]
-    for k in range(1, COLS):
-        peers.append((r, lax.rem(c + k, COLS)))
+    peers = [at_z(1), at_z(-1), x_pair, sibling, x_far, at_y(1), at_y(2), at_y(3)]
     for peer in peers:
         pl.semaphore_signal(barrier, inc=1, device_id=peer, device_id_type=MESH)
     pl.semaphore_wait(barrier, len(peers))
@@ -114,31 +117,38 @@
     ring = {}
     for h in range(HALVES):
         for k in range(4):
-            if k < 3:
-                src_f = s["own"].at[h] if k == 0 else fwd[h][k - 1]
-                src_b = s["own"].at[h] if k == 0 else bwd[h][k - 1]
-                dst_f, dst_b = fwd[h][k], bwd[h][k]
-            else:
-                src_f, dst_f = fwd[h][2].at[pl.ds(0, 2)], opp[h].at[pl.ds(0, 2)]
-                src_b, dst_b = bwd[h][2].at[pl.ds(2, 2)], opp[h].at[pl.ds(2, 2)]
-            ring[h, 0, k] = sems.copy(src_f, dst_f, at_z(1))
-            ring[h, 1, k] = sems.copy(src_b, dst_b, at_z(-1))
+            for q in range(2):
+                part = pl.ds(2 * q, 2)
+                for way, chain in ((0, fwd[h]), (1, bwd[h])):
+                    if k == 3 and q != way:
+                        continue
+                    src = s["own"].at[h] if k == 0 else chain[k - 1]
+                    dst = chain[k] if k < 3 else opp[h]
+                    ring[h, way, k, q] = sems.copy(
+                        src.at[part], dst.at[part], at_z(1 - 2 * way)
+                    )
     lists_copy = sems.copy(s["lists_out"], s["lists_in"], x_pair)
 
-    for h in range(HALVES):
-        ring[h, 0, 0].start()
-        ring[h, 1, 0].start()
     lists_copy.start()
+
+    def send(h, q):
+        for way in range(2):
+            ring[h, way, 0, q].start()
+
+    send(0, 0)
+    send(0, 1)
+    send(1, 0)
+    send(1, 1)
 
     pair_copies = {}
 
     def select(h, slot, block, dist):
         owner = x_lo * Z + z_at(dist)
         for j in range(CAP):
-            mine = jnp.maximum(lists_ref[0, owner * CAP + j], 0)
+            mine = jnp.maximum(lists_ref[j, owner], 0)
             oper[h][owner * CAP + j] = block[mine]
         for j in range(CAP):
-            theirs = jnp.maximum(s["lists_smem"][0, owner * CAP + j], 0)
+            theirs = jnp.maximum(s["lists_smem"][j, owner], 0)
             s[f"pair{h}"][slot * CAP + j] = block[theirs]
         cp = sems.copy(
             s[f"pair{h}"].at[pl.ds(slot * CAP, CAP)],
@@ -169,6 +179,44 @@
     for h in range(HALVES):
         s[f"sums{h}"][TILES] = jnp.zeros((TILE, TILE), F32)
 
+    ones = jnp.ones((16, TILE), BF16)
+
+    def prepare(lo, hi):
+        for k in range(CHUNKS):
+            if lo <= k * per < hi:
+                tile_copies[k].wait()
+
+        def body(t, _):
+            block = s["tiles32"][t].astype(F32).astype(BF16)
+            s["blocks"][t] = block
+            sums = lax.dot_general(
+                ones, block, (((1,), (1,)), ((), ())), preferred_element_type=F32
+            )
+            s["degs"][pl.ds(t, 1), :] = sums[0:1, :]
+            return 0
+
+        lax.fori_loop(lo, hi, body, 0, unroll=True)
+
+    def arrive(h, k, q):
+        for way in range(2):
+            if (h, way, k, q) in ring:
+                ring[h, way, k, q].wait_recv()
+            if (h, way, k + 1, q) in ring:
+                ring[h, way, k + 1, q].start()
+
+    def cross(h, k):
+        if k < 3:
+            select(h, 1 + k, fwd[h][k], -(k + 1))
+            select(h, 4 + k, bwd[h][k], k + 1)
+        else:
+            select(h, 7, opp[h], 4)
+
+    def base(i):
+        mixed = jnp.dot(s["own"][0, i], s["ws"][0:TILE, :], preferred_element_type=F32)
+        mixed += jnp.dot(s["own"][1, i], s["ws"][TILE : 2 * TILE, :], preferred_element_type=F32)
+        s["mixed"][i] = mixed + bias_ref[...]
+
+    prepare(0, 12)
     lists_copy.wait_recv()
     smem_copy = pltpu.make_async_copy(
         s["lists_in"], s["lists_smem"], local.at[HALVES + CHUNKS + 1]
@@ -178,62 +226,81 @@
     for h in range(HALVES):
         select(h, 0, s["own"].at[h], 0)
 
-    ones = jnp.ones((16, TILE), BF16)
-
-    def prepare(k):
-        tile_copies[k].wait()
-
-        def body(t, _):
-            block = s["tiles32"][t].astype(F32).astype(BF16)
-            s["blocks"][t] = block
-            sums = lax.dot_general(
-                ones, block, (((1,), (1,)), ((), ())), preferred_element_type=F32
-            )
-            s["degs"][pl.ds(t, 1), :] = sums[0:1, :]
-            return 0
-
-        lax.fori_loop(k * per, (k + 1) * per, body, 0, unroll=4)
-
-    def arrive(h, k):
-        for way in (0, 1):
-            ring[h, way, k].wait_recv()
-            if k < 3:
-                ring[h, way, k + 1].start()
-        if k < 3:
-            select(h, 1 + k, fwd[h][k], -(k + 1))
-            select(h, 4 + k, bwd[h][k], k + 1)
-        else:
-            select(h, 7, opp[h], 4)
-
-    def base(i):
-        mixed = jnp.dot(s["own"][0, i], ws_ref[0:TILE, :], preferred_element_type=F32)
-        mixed += jnp.dot(s["own"][1, i], ws_ref[TILE : 2 * TILE, :], preferred_element_type=F32)
-        s["mixed"][i] = mixed + bias_ref[...]
-
-    for k in range(4):
-        prepare(k)
-        for h in range(HALVES):
-            arrive(h, k)
-        base(k)
-
-    q = lax.broadcasted_iota(jnp.int32, (TILE, TILE), 0)
-    panel = jnp.where(lax.rem(q, 8) < 4, (q // 8) * 4 + lax.rem(q, 8), -2)
-    hot = (panel == row_l).astype(F32).astype(BF16)
-    s["degs"][TILES:TILE, :] = jnp.zeros((TILE - TILES, TILE), F32)
-    degs = jnp.dot(hot, s["degs"][...].astype(BF16), preferred_element_type=F32)
-    s["deg_out"][...] = degs.reshape(COLS, 8, TILE)
-    deg_copies = []
-    for k in range(1, COLS):
-        to = lax.rem(c + k, COLS)
-        cp = sems.copy(s["deg_out"].at[to], s["deg_in"].at[k - 1], (r, to))
-        cp.start()
-        deg_copies.append(cp)
+    deg = {}
+
+    def degree0():
+        q = lax.broadcasted_iota(jnp.int32, (TILE, TILE), 0)
+        b = q // 8
+        owner = lax.rem(b, 4) * 4 + lax.rem(b // 4, 2) * 2 + b // 8
+        panel = jnp.where(lax.rem(q, 8) < PANELS, owner * PANELS + lax.rem(q, 8), -2)
+        hot = (panel == row_l).astype(F32).astype(BF16)
+        s["degs"][TILES:TILE, :] = jnp.zeros((TILE - TILES, TILE), F32)
+        degs = jnp.dot(hot, s["degs"][...].astype(BF16), preferred_element_type=F32)
+        s["deg0_out"][...] = degs.reshape(2, 2, Y, 8, TILE)
+        deg[0] = sems.copy(s["deg0_out"].at[1 - core], s["deg0_in"], sibling)
+        deg[0].start()
+
+    def degree1():
+        deg[0].wait_recv()
+        s["deg1_out"][...] = s["deg0_out"][core] + s["deg0_in"][...]
+        deg[1] = sems.copy(s["deg1_out"].at[1 - x_hi], s["deg1_in"], x_far)
+        deg[1].start()
+
+    def degree2():
+        deg[1].wait_recv()
+        s["deg2_out"][...] = s["deg1_out"][x_hi] + s["deg1_in"][...]
+        for dy in range(1, Y):
+            to = lax.rem(y + dy, Y)
+            deg[2, dy] = sems.copy(s["deg2_out"].at[to], s["deg2_in"].at[dy - 1], at_y(dy))
+            deg[2, dy].start()
+
+    def degree3():
+        total = s["deg2_out"][y]
+        for dy in range(1, Y):
+            deg[2, dy].wait_recv()
+            total += s["deg2_in"][dy - 1]
+        total = jnp.maximum(total, 1.0)
+        wide = jnp.transpose(jnp.concatenate([total] * 16, axis=0))
+        for i in range(PANELS):
+            s["deg"][i] = jnp.broadcast_to(wide[:, i : i + 1], (TILE, TILE))
+
+    def hop(h, k):
+        arrive(h, k, 0)
+        arrive(h, k, 1)
+        cross(h, k)
+
+    hop(0, 0)
+    prepare(12, 36)
+    hop(1, 0)
+    prepare(36, 60)
+    hop(0, 1)
+    prepare(60, 84)
+    hop(1, 1)
+    prepare(84, 96)
+    degree0()
+    arrive(0, 2, 0)
+    arrive(0, 2, 1)
+    cross(0, 2)
+    arrive(1, 2, 0)
+    arrive(0, 3, 0)
+    arrive(0, 3, 1)
+    cross(0, 3)
+    arrive(1, 2, 1)
+    cross(1, 2)
+    arrive(1, 3, 0)
+    arrive(1, 3, 1)
+    cross(1, 3)
+    for cp in weight_copies:
+        cp.wait()
+    for i in range(PANELS):
+        base(i)
 
     meta_copy.wait()
 
-    def products(h):
-        for slot in range(8):
-            pair_copies[h, slot].wait_recv()
+    def products(h, lo, hi):
+        if lo == 0:
+            for slot in range(8):
+                pair_copies[h, slot].wait_recv()
         sums = s[f"sums{h}"]
 
         def body(t, _):
@@ -243,7 +310,7 @@
             sums[t] = value + sums[s["meta_smem"][0, t]]
             return 0
 
-        lax.fori_loop(0, TILES, body, 0, unroll=4)
+        lax.fori_loop(lo, hi, body, 0, unroll=4)
 
     def owner_col(dy, dx, which):
         hi = x_hi if dx == 0 else 1 - x_hi
@@ -360,26 +427,18 @@
                     total += s[f"y2_in{h}"][dy - 1, i - n].astype(F32)
             mean = (total / s["deg"][i]).astype(BF16)
             s["mixed"][i] += jnp.dot(
-                mean, wn_ref[h * TILE : (h + 1) * TILE, :], preferred_element_type=F32
+                mean, s["wn"][h * TILE : (h + 1) * TILE, :], preferred_element_type=F32
             )
 
-    def degree():
-        total = s["deg_out"][c]
-        for k in range(1, COLS):
-            deg_copies[k - 1].wait_recv()
-            total += s["deg_in"][k - 1]
-        total = jnp.maximum(total, 1.0)
-        wide = jnp.transpose(jnp.concatenate([total] * 16, axis=0))
-        for i in range(PANELS):
-            s["deg"][i] = jnp.broadcast_to(wide[:, i : i + 1], (TILE, TILE))
-
-    products(0)
+    products(0, 0, 96)
     exchange(0)
-    degree()
+    degree1()
     first(0)
-    products(1)
+    products(1, 0, 96)
     exchange(1)
+    degree2()
     first(1)
+    degree3()
     second(0)
     second(1)
     third(0)
@@ -393,15 +452,21 @@
 def scratch_spec():
     panel = lambda *lead: pltpu.VMEM((*lead, TILE, TILE), BF16)
     spec = {
-        "send_sem": pltpu.SemaphoreType.DMA((96,)),
-        "recv_sem": pltpu.SemaphoreType.DMA((96,)),
-        "local_sem": pltpu.SemaphoreType.DMA((HALVES + CHUNKS + 2,)),
+        "send_sem": pltpu.SemaphoreType.DMA((112,)),
+        "recv_sem": pltpu.SemaphoreType.DMA((112,)),
+        "local_sem": pltpu.SemaphoreType.DMA((HALVES + CHUNKS + 4,)),
         "own": panel(HALVES, PANELS),
+        "ws": pltpu.VMEM((2 * TILE, 2 * TILE), BF16),
+        "wn": pltpu.VMEM((2 * TILE, 2 * TILE), BF16),
         "tiles32": pltpu.VMEM((TILES, TILE, TILE), jnp.int32),
         "blocks": panel(TILES),
         "degs": pltpu.VMEM((TILE, TILE), F32),
-        "deg_out": pltpu.VMEM((COLS, 8, TILE), F32),
-        "deg_in": pltpu.VMEM((COLS - 1, 8, TILE), F32),
+        "deg0_out": pltpu.VMEM((2, 2, Y, 8, TILE), F32),
+        "deg0_in": pltpu.VMEM((2, Y, 8, TILE), F32),
+        "deg1_out": pltpu.VMEM((2, Y, 8, TILE), F32),
+        "deg1_in": pltpu.VMEM((Y, 8, TILE), F32),
+        "deg2_out": pltpu.VMEM((Y, 8, TILE), F32),
+        "deg2_in": pltpu.VMEM((Y - 1, 8, TILE), F32),
         "deg": pltpu.VMEM((PANELS, TILE, TILE), F32),
         "rows": pltpu.VMEM((8, TILE), jnp.int32),
         "meta": pltpu.VMEM((8, TILE), jnp.int32),
@@ -445,11 +510,11 @@
     vmem = pl.BlockSpec(memory_space=pltpu.VMEM)
     smem = pl.BlockSpec(memory_space=pltpu.SMEM)
     hbm = pl.BlockSpec(memory_space=pl.ANY)
-    lists = panel_lists.reshape(1, ROWS * CAP)
+    lists = panel_lists[0, 0].T
     return pl.pallas_call(
         kernel,
         out_shape=jax.ShapeDtypeStruct((PANELS * TILE, 2 * TILE), BF16),
-        in_specs=[hbm, hbm, vmem, smem, smem, smem, vmem, vmem, vmem, vmem],
+        in_specs=[hbm, hbm, vmem, smem, smem, smem, vmem, hbm, hbm, vmem],
         out_specs=vmem,
         scratch_shapes=list(scratch_spec().values()),
         compiler_params=pltpu.CompilerParams(

time: 73.9 us -> 66.2 us (0.90)
  Pallas kernels: 70.1 us -> 63.8 us
  local copies, waits for them, and re-layouts: 3.03 us -> 1.67 us
    pallas_call x1, Pallas kernels: 70.1 us -> 63.8 us  [shards(): pl.pallas_call(kernel, out_shape=jax.ShapeDtypeStruct((PANELS * TILE, 2 *...]
    unnamed x2 -> x1, local copies, waits for them, and re-layouts: 2.43 us -> 1.67 us
where the time goes in v2:
time: 66.2 us; the launch traced here: 66.1 us
  Pallas kernels  63.8 us (96%)
  local copies, waits for them, and re-layouts  1.67 us (3%)
    pallas_call x1, Pallas kernels, shards(): pl.pallas_call(kernel, out_shape=jax.ShapeDtypeStruct((PANELS * TILE, 2 *...  63.8 us
    unnamed x1, local copies, waits for them, and re-layouts  1.67 us

profile of v2, /device:TPU:1, one launch (start us, length us, event | category | flops | bytes accessed | tf_op | source)
XLA Modules:
  0.0 66.1 jit_solution(7644758287550492725)
XLA Ops:
  0.7 63.8 %sage.1 = bf16[512,256]{1,0:T(8,128)(2,1)} custom-call(bf16[4,128,256]{2,1,0:T(8,128)(2,1)} %bitcast.9, s32[96,128,128]{2,1,0:T(8,128)} %bitcast.8, s32[1,96]{1,0:T(1,128)} %bitcast.13, s32[1,96]{1,0:T(1,128)} %bitcast.14, s32[1,1]{1,0:T(1,128)S(6)} %copy.11.count_ref, s32[2,16]{1,0:T(2,128)} %bitcast.10, s32[2,16]{1,0:T(2,128)} %bitcast.11, ...), custom_call_target="tpu_custom_call" | custom-call | tf_op jit(solution)/shard_map/sage/pallas_call | solution.py:514
  64.4 1.7 %copy.12 = bf16[512,256]{1,0:T(8,128)(2,1)} copy(bf16[512,256]{1,0:T(8,128)(2,1)} %sage.1) | data formatting | bytes 524288

commit v3 on v2

--- a/solution.py
+++ b/solution.py
@@ -46,14 +46,13 @@
 def kernel(
     feat_ref,
     tiles_ref,
-    rows_ref,
-    cols_ref,
-    count_ref,
-    lists_ref,
-    lists_vec_ref,
-    ws_ref,
-    wn_ref,
-    bias_ref,
+    rows_hbm,
+    cols_hbm,
+    count_hbm,
+    lists_hbm,
+    ws_hbm,
+    wn_hbm,
+    bias_hbm,
     out_ref,
     *scratch,
 ):
@@ -69,7 +68,7 @@
         return (x_lo * Z + z_at(d), c)
 
     def at_y(d):
-        return (r, lax.rem(c + 4 * d, COLS))
+        return (r, lax.rem(c + 4 * d + COLS, COLS))
 
     x_pair = ((1 - x_lo) * Z + z, c)
     x_far = (r, c + 2 - 4 * x_hi)
@@ -83,6 +82,22 @@
         )
         cp.start()
         own_copies.append(cp)
+    small_copies, weight_copies = [], []
+    for k, (src, dst) in enumerate(
+        (
+            (lists_hbm, s["lists_vec"]),
+            (lists_hbm, s["lists"]),
+            (rows_hbm, s["rows_vec"]),
+            (count_hbm, s["count"]),
+            (cols_hbm, s["cols"]),
+            (bias_hbm, s["bias"]),
+            (ws_hbm, s["ws"]),
+            (wn_hbm, s["wn"]),
+        )
+    ):
+        cp = pltpu.make_async_copy(src, dst, local.at[HALVES + CHUNKS + 2 + k])
+        cp.start()
+        (small_copies if k < 5 else weight_copies).append(cp)
     per = TILES // CHUNKS
     tile_copies = []
     for k in range(CHUNKS):
@@ -92,13 +107,6 @@
         )
         cp.start()
         tile_copies.append(cp)
-    weight_copies = []
-    for k, (src, dst) in enumerate(((ws_ref, s["ws"]), (wn_ref, s["wn"]))):
-        cp = pltpu.make_async_copy(src, dst, local.at[HALVES + CHUNKS + 2 + k])
-        cp.start()
-        weight_copies.append(cp)
-    s["lists_out"][...] = jnp.zeros((8, TILE), jnp.int32)
-    s["lists_out"][0:CAP, 0:ROWS] = lists_vec_ref[...]
 
     barrier = pltpu.get_barrier_semaphore()
     peers = [at_z(1), at_z(-1), x_pair, sibling, x_far, at_y(1), at_y(2), at_y(3)]
@@ -129,7 +137,9 @@
                     )
     lists_copy = sems.copy(s["lists_out"], s["lists_in"], x_pair)
 
-    lists_copy.start()
+    for cp in small_copies:
+        cp.wait()
+    lists_ref, cols_ref = s["lists"], s["cols"]
 
     def send(h, q):
         for way in range(2):
@@ -137,6 +147,9 @@
 
     send(0, 0)
     send(0, 1)
+    s["lists_out"][...] = jnp.zeros((8, TILE), jnp.int32)
+    s["lists_out"][0:CAP, 0:ROWS] = s["lists_vec"][...]
+    lists_copy.start()
     send(1, 0)
     send(1, 1)
 
@@ -158,11 +171,11 @@
         cp.start()
         pair_copies[h, slot] = cp
 
-    live = count_ref[0, 0]
+    live = s["count"][0, 0]
     lane = lax.broadcasted_iota(jnp.int32, (TILE, TILE), 1)
     sub = lax.broadcasted_iota(jnp.int32, (TILE, TILE), 0)
     s["rows"][...] = jnp.full((8, TILE), -1, jnp.int32)
-    s["rows"][0:1, 0:TILES] = rows_ref[...]
+    s["rows"][0:1, 0:TILES] = s["rows_vec"][...]
     row_l = jnp.broadcast_to(s["rows"][0:1, :], (TILE, TILE))
     row_l = jnp.where(lane < live, row_l, -1)
     row_s = jnp.transpose(row_l.astype(F32)).astype(jnp.int32)
@@ -214,7 +227,7 @@
     def base(i):
         mixed = jnp.dot(s["own"][0, i], s["ws"][0:TILE, :], preferred_element_type=F32)
         mixed += jnp.dot(s["own"][1, i], s["ws"][TILE : 2 * TILE, :], preferred_element_type=F32)
-        s["mixed"][i] = mixed + bias_ref[...]
+        s["mixed"][i] = mixed + s["bias"][...]
 
     prepare(0, 12)
     lists_copy.wait_recv()
@@ -264,37 +277,36 @@
         for i in range(PANELS):
             s["deg"][i] = jnp.broadcast_to(wide[:, i : i + 1], (TILE, TILE))
 
-    def hop(h, k):
-        arrive(h, k, 0)
-        arrive(h, k, 1)
-        cross(h, k)
-
-    hop(0, 0)
+    arrive(0, 0, 0)
+    arrive(0, 0, 1)
+    cross(0, 0)
     prepare(12, 36)
-    hop(1, 0)
+    arrive(1, 0, 0)
+    arrive(1, 0, 1)
+    cross(1, 0)
     prepare(36, 60)
-    hop(0, 1)
+    arrive(0, 1, 0)
+    arrive(0, 1, 1)
+    cross(0, 1)
     prepare(60, 84)
-    hop(1, 1)
+    arrive(1, 1, 0)
+    arrive(1, 1, 1)
+    cross(1, 1)
     prepare(84, 96)
     degree0()
     arrive(0, 2, 0)
     arrive(0, 2, 1)
     cross(0, 2)
-    arrive(1, 2, 0)
     arrive(0, 3, 0)
     arrive(0, 3, 1)
     cross(0, 3)
+    arrive(1, 2, 0)
     arrive(1, 2, 1)
     cross(1, 2)
-    arrive(1, 3, 0)
-    arrive(1, 3, 1)
-    cross(1, 3)
     for cp in weight_copies:
         cp.wait()
     for i in range(PANELS):
         base(i)
-
     meta_copy.wait()
 
     def products(h, lo, hi):
@@ -310,7 +322,7 @@
             sums[t] = value + sums[s["meta_smem"][0, t]]
             return 0
 
-        lax.fori_loop(lo, hi, body, 0, unroll=4)
+        lax.fori_loop(lo, hi, body, 0, unroll=24)
 
     def owner_col(dy, dx, which):
         hi = x_hi if dx == 0 else 1 - x_hi
@@ -341,44 +353,52 @@
         j = dy * 2 + dx
         return partial(h, dy, dx, core, i) + s["swap_in"][h, j * PANELS + i].astype(F32)
 
-    stage1, stage2 = {}, {}
+    stage1, stage2, arrived = {}, {}, set()
+
+    def need(h, dy):
+        for dx in (1, 0):
+            if (h, dy, dx) not in arrived:
+                arrived.add((h, dy, dx))
+                swap[h, dy * 2 + dx].wait_recv()
+
+    def post(stage, key, out, into, device):
+        cp = sems.copy(out, into, device)
+        cp.start()
+        stage[key] = cp
 
     def first(h):
         n = YFIRST[h]
         m = PANELS - n
-        arrived = set()
-
-        def need(dy, dx):
-            if (dy, dx) not in arrived:
-                arrived.add((dy, dx))
-                swap[h, dy * 2 + dx].wait_recv()
-
-        for dy in (2, 1, 3):
-            need(dy, 1)
-            need(dy, 0)
-            if n:
-                for dx in (1, 0):
+        far_out, far_in = s[f"far_out{h}"], s[f"far_in{h}"]
+        y1_out, y1_in = s[f"y1_out{h}"], s[f"y1_in{h}"]
+        for dy in (2, 1, 3, 0):
+            need(h, dy)
+            if dy == 2:
+                for side in range(2):
                     for i in range(n):
-                        s[f"y1_out{h}"][dy - 1, dx * n + i] = both(h, dy, dx, i).astype(BF16)
-                cp = sems.copy(
-                    s[f"y1_out{h}"].at[dy - 1], s[f"y1_in{h}"].at[dy - 1], at_y(dy)
-                )
-                cp.start()
-                stage1[h, dy] = cp
+                        far_out[side, i] = both(h, 2, side, i).astype(BF16)
+                    post(stage1, (h, "far", side), far_out.at[side], far_in.at[side], at_y(1 - 2 * side))
+            elif dy:
+                side = dy // 2
+                dx = 1 - side
+                for i in range(n):
+                    y1_out[side, dx, i] = both(h, dy, dx, i).astype(BF16)
+                post(stage1, (h, "y", side, dx), y1_out.at[side, dx], y1_in.at[side, dx], at_y(1 - 2 * side))
+            for i in range(m):
+                s[f"x1_out{h}"][dy, i] = both(h, dy, 1, n + i).astype(BF16)
             if m:
-                for i in range(m):
-                    s[f"x1_out{h}"][dy, i] = both(h, dy, 1, n + i).astype(BF16)
-                cp = sems.copy(s[f"x1_out{h}"].at[dy], s[f"x1_in{h}"].at[dy], x_far)
-                cp.start()
-                stage1[h, "x", dy] = cp
-        need(0, 1)
-        need(0, 0)
-        if m:
-            for i in range(m):
-                s[f"x1_out{h}"][0, i] = both(h, 0, 1, n + i).astype(BF16)
-            cp = sems.copy(s[f"x1_out{h}"].at[0], s[f"x1_in{h}"].at[0], x_far)
-            cp.start()
-            stage1[h, "x", 0] = cp
+                post(stage1, (h, "x", dy), s[f"x1_out{h}"].at[dy], s[f"x1_in{h}"].at[dy], x_far)
+
+    def middle(h):
+        n = YFIRST[h]
+        y1_out, y1_in = s[f"y1_out{h}"], s[f"y1_in{h}"]
+        for side in range(2):
+            stage1[h, "far", side].wait_recv()
+            dy, dx = 1 + 2 * side, side
+            for i in range(n):
+                total = both(h, dy, dx, i) + s[f"far_in{h}"][side, i].astype(F32)
+                y1_out[side, dx, i] = total.astype(BF16)
+            post(stage1, (h, "y", side, dx), y1_out.at[side, dx], y1_in.at[side, dx], at_y(1 - 2 * side))
 
     def second(h):
         n = YFIRST[h]
@@ -389,22 +409,15 @@
                 for i in range(m):
                     total = both(h, dy, 0, n + i) + s[f"x1_in{h}"][dy, i].astype(F32)
                     s[f"y2_out{h}"][dy - 1, i] = total.astype(BF16)
-                cp = sems.copy(
-                    s[f"y2_out{h}"].at[dy - 1], s[f"y2_in{h}"].at[dy - 1], at_y(dy)
-                )
-                cp.start()
-                stage2[h, dy] = cp
-        if n:
-            for dy in (2, 1, 3):
-                stage1[h, dy].wait_recv()
-            for i in range(n):
-                total = both(h, 0, 1, i)
-                for dy in (2, 1, 3):
-                    total += s[f"y1_in{h}"][dy - 1, n + i].astype(F32)
-                s[f"x2_out{h}"][i] = total.astype(BF16)
-            cp = sems.copy(s[f"x2_out{h}"], s[f"x2_in{h}"], x_far)
-            cp.start()
-            stage2[h, "x"] = cp
+                post(stage2, (h, dy), s[f"y2_out{h}"].at[dy - 1], s[f"y2_in{h}"].at[dy - 1], at_y(dy))
+        for side in range(2):
+            stage1[h, "y", side, 1].wait_recv()
+        for i in range(n):
+            total = both(h, 0, 1, i)
+            for side in range(2):
+                total += s[f"y1_in{h}"][side, 1, i].astype(F32)
+            s[f"x2_out{h}"][i] = total.astype(BF16)
+        post(stage2, (h, "x"), s[f"x2_out{h}"], s[f"x2_in{h}"], x_far)
 
     def third(h):
         n = YFIRST[h]
@@ -413,13 +426,14 @@
             stage1[h, "x", 0].wait_recv()
             for dy in (2, 1, 3):
                 stage2[h, dy].wait_recv()
-        if n:
-            stage2[h, "x"].wait_recv()
+        for side in range(2):
+            stage1[h, "y", side, 0].wait_recv()
+        stage2[h, "x"].wait_recv()
         for i in range(PANELS):
             total = both(h, 0, 0, i)
             if i < n:
-                for dy in (2, 1, 3):
-                    total += s[f"y1_in{h}"][dy - 1, i].astype(F32)
+                for side in range(2):
+                    total += s[f"y1_in{h}"][side, 0, i].astype(F32)
                 total += s[f"x2_in{h}"][i].astype(F32)
             else:
                 total += s[f"x1_in{h}"][0, i - n].astype(F32)
@@ -430,15 +444,22 @@
                 mean, s["wn"][h * TILE : (h + 1) * TILE, :], preferred_element_type=F32
             )
 
-    products(0, 0, 96)
+    products(0, 0, 48)
+    arrive(1, 3, 0)
+    arrive(1, 3, 1)
+    cross(1, 3)
+    products(0, 48, 96)
     exchange(0)
     degree1()
     first(0)
-    products(1, 0, 96)
+    products(1, 0, 48)
+    middle(0)
+    products(1, 48, 96)
     exchange(1)
     degree2()
     first(1)
     degree3()
+    middle(1)
     second(0)
     second(1)
     third(0)
@@ -454,8 +475,14 @@
     spec = {
         "send_sem": pltpu.SemaphoreType.DMA((112,)),
         "recv_sem": pltpu.SemaphoreType.DMA((112,)),
-        "local_sem": pltpu.SemaphoreType.DMA((HALVES + CHUNKS + 4,)),
+        "local_sem": pltpu.SemaphoreType.DMA((HALVES + CHUNKS + 10,)),
         "own": panel(HALVES, PANELS),
+        "lists_vec": pltpu.VMEM((CAP, ROWS), jnp.int32),
+        "lists": pltpu.SMEM((CAP, ROWS), jnp.int32),
+        "rows_vec": pltpu.VMEM((1, TILES), jnp.int32),
+        "count": pltpu.SMEM((1, 1), jnp.int32),
+        "cols": pltpu.SMEM((1, TILES), jnp.int32),
+        "bias": pltpu.VMEM((1, 2 * TILE), F32),
         "ws": pltpu.VMEM((2 * TILE, 2 * TILE), BF16),
         "wn": pltpu.VMEM((2 * TILE, 2 * TILE), BF16),
         "tiles32": pltpu.VMEM((TILES, TILE, TILE), jnp.int32),
@@ -488,11 +515,10 @@
         spec[f"sums{h}"] = pltpu.VMEM((TILES + 1, TILE, TILE), F32)
         n = YFIRST[h]
         m = PANELS - n
-        if n:
-            spec[f"y1_out{h}"] = panel(3, 2 * n)
-            spec[f"y1_in{h}"] = panel(3, 2 * n)
-            spec[f"x2_out{h}"] = panel(n)
-            spec[f"x2_in{h}"] = panel(n)
+        for end in ("out", "in"):
+            spec[f"far_{end}{h}"] = panel(2, n)
+            spec[f"y1_{end}{h}"] = panel(2, 2, n)
+            spec[f"x2_{end}{h}"] = panel(n)
         if m:
             spec[f"x1_out{h}"] = panel(4, m)
             spec[f"x1_in{h}"] = panel(4, m)
@@ -508,13 +534,12 @@
     features, tiles, tile_rows, tile_cols, tile_count, panel_lists, self_weight, neigh_weight, bias
 ):
     vmem = pl.BlockSpec(memory_space=pltpu.VMEM)
-    smem = pl.BlockSpec(memory_space=pltpu.SMEM)
-    hbm = pl.BlockSpec(memory_space=pl.ANY)
+    hbm = pl.BlockSpec(memory_space=pltpu.HBM)
     lists = panel_lists[0, 0].T
     return pl.pallas_call(
         kernel,
         out_shape=jax.ShapeDtypeStruct((PANELS * TILE, 2 * TILE), BF16),
-        in_specs=[hbm, hbm, vmem, smem, smem, smem, vmem, hbm, hbm, vmem],
+        in_specs=[hbm] * 9,
         out_specs=vmem,
         scratch_shapes=list(scratch_spec().values()),
         compiler_params=pltpu.CompilerParams(
@@ -527,7 +552,6 @@
         tile_rows[0],
         tile_cols[0],
         tile_count,
-        lists,
         lists,
         self_weight,
         neigh_weight,

time: 66.2 us -> 60.3 us (0.911)
  the two profiles are of different devices: /device:TPU:1 before, /device:TPU:24 now
where the time goes in v3:
time: 60.3 us; the launch traced here: 60.2 us
  Pallas kernels  57.8 us (96%)
  local copies, waits for them, and re-layouts  1.67 us (3%)
  between operations  0.66 us (1%)
    pallas_call x1, Pallas kernels, shards(): pl.pallas_call(kernel, out_shape=jax.ShapeDtypeStruct((PANELS * TILE, 2 *...  57.8 us
    unnamed x1, local copies, waits for them, and re-layouts  1.67 us

profile of v3, /device:TPU:24, one launch (start us, length us, event | category | flops | bytes accessed | tf_op | source)
XLA Modules:
  0.0 60.2 jit_solution(6313132895271039305)
XLA Ops:
  0.7 57.8 %sage.1 = bf16[512,256]{1,0:T(8,128)(2,1)} custom-call(bf16[4,128,256]{2,1,0:T(8,128)(2,1)} %bitcast.9, s32[96,128,128]{2,1,0:T(8,128)} %bitcast.8, s32[1,96]{1,0:T(1,128)} %bitcast.12, s32[1,96]{1,0:T(1,128)} %bitcast.13, s32[1,1]{1,0:T(1,128)S(6)} %copy.11.count_hbm, s32[2,16]{1,0:T(2,128)} %bitcast.10, bf16[256,256]{1,0:T(8,128)(2,1)} %ws_hbm.1, ...), custom_call_target="tpu_custom_call" | custom-call | tf_op jit(solution)/shard_map/sage/pallas_call | solution.py:539
  58.5 1.7 %copy.12 = bf16[512,256]{1,0:T(8,128)(2,1)} copy(bf16[512,256]{1,0:T(8,128)(2,1)} %sage.1) | data formatting | bytes 524288

commit v4 on v3

--- a/solution.py
+++ b/solution.py
@@ -41,6 +41,11 @@
         )
         self.copies.append(c)
         return c
+
+    def sent(self):
+        for c in self.copies:
+            c.wait_send()
+        self.copies = []
 
 
 def kernel(
@@ -73,6 +78,11 @@
     x_pair = ((1 - x_lo) * Z + z, c)
     x_far = (r, c + 2 - 4 * x_hi)
     sibling = (r, c + 1 - 2 * core)
+
+    barrier = pltpu.get_barrier_semaphore()
+    peers = [at_z(1), at_z(-1), x_pair, sibling, x_far, at_y(1), at_y(2), at_y(3)]
+    for peer in peers:
+        pl.semaphore_signal(barrier, inc=1, device_id=peer, device_id_type=MESH)
 
     local = s["local_sem"]
     own_copies = []
@@ -99,19 +109,7 @@
         cp.start()
         (small_copies if k < 5 else weight_copies).append(cp)
     per = TILES // CHUNKS
-    tile_copies = []
-    for k in range(CHUNKS):
-        part = pl.ds(k * per, per)
-        cp = pltpu.make_async_copy(
-            tiles_ref.at[part], s["tiles32"].at[part], local.at[HALVES + k]
-        )
-        cp.start()
-        tile_copies.append(cp)
-
-    barrier = pltpu.get_barrier_semaphore()
-    peers = [at_z(1), at_z(-1), x_pair, sibling, x_far, at_y(1), at_y(2), at_y(3)]
-    for peer in peers:
-        pl.semaphore_signal(barrier, inc=1, device_id=peer, device_id_type=MESH)
+
     pl.semaphore_wait(barrier, len(peers))
 
     sems = Sems(s["send_sem"], s["recv_sem"])
@@ -152,6 +150,14 @@
     lists_copy.start()
     send(1, 0)
     send(1, 1)
+    tile_copies = []
+    for k in range(CHUNKS):
+        part = pl.ds(k * per, per)
+        cp = pltpu.make_async_copy(
+            tiles_ref.at[part], s["tiles32"].at[part], local.at[HALVES + k]
+        )
+        cp.start()
+        tile_copies.append(cp)
 
     pair_copies = {}
 
@@ -353,7 +359,7 @@
         j = dy * 2 + dx
         return partial(h, dy, dx, core, i) + s["swap_in"][h, j * PANELS + i].astype(F32)
 
-    stage1, stage2, arrived = {}, {}, set()
+    stage1, stage2, arrived, hidden_copies = {}, {}, set(), []
 
     def need(h, dy):
         for dx in (1, 0):
@@ -422,14 +428,13 @@
     def third(h):
         n = YFIRST[h]
         m = PANELS - n
-        if m:
-            stage1[h, "x", 0].wait_recv()
-            for dy in (2, 1, 3):
-                stage2[h, dy].wait_recv()
-        for side in range(2):
-            stage1[h, "y", side, 0].wait_recv()
-        stage2[h, "x"].wait_recv()
-        for i in range(PANELS):
+        ends = [(stage1, (h, "x", 0))] + [(stage2, (h, dy)) for dy in (2, 1, 3)] if m else []
+        for i in (*range(n, PANELS), *range(n)):
+            if i == 0:
+                ends = [(stage1, (h, "y", side, 0)) for side in range(2)] + [(stage2, (h, "x"))]
+            for stage, key in ends:
+                stage[key].wait_recv()
+            ends = []
             total = both(h, 0, 0, i)
             if i < n:
                 for side in range(2):
@@ -440,14 +445,22 @@
                 for dy in (2, 1, 3):
                     total += s[f"y2_in{h}"][dy - 1, i - n].astype(F32)
             mean = (total / s["deg"][i]).astype(BF16)
-            s["mixed"][i] += jnp.dot(
+            mixed = s["mixed"][i] + jnp.dot(
                 mean, s["wn"][h * TILE : (h + 1) * TILE, :], preferred_element_type=F32
             )
+            if h < HALVES - 1:
+                s["mixed"][i] = mixed
+            else:
+                s["hidden"][i] = jnp.maximum(mixed, 0.0).astype(BF16)
+                cp = pltpu.make_async_copy(s["hidden"].at[i], out_ref.at[i], local.at[i])
+                cp.start()
+                hidden_copies.append(cp)
 
     products(0, 0, 48)
     arrive(1, 3, 0)
     arrive(1, 3, 1)
     cross(1, 3)
+    gathered, sems.copies = sems.copies, []
     products(0, 48, 96)
     exchange(0)
     degree1()
@@ -458,16 +471,20 @@
     exchange(1)
     degree2()
     first(1)
+    for cp in gathered:
+        cp.wait_send()
     degree3()
     middle(1)
     second(0)
+    reducing, sems.copies = sems.copies, []
     second(1)
     third(0)
+    for cp in reducing:
+        cp.wait_send()
     third(1)
-    for i in range(PANELS):
-        out_ref[pl.ds(i * TILE, TILE), :] = jnp.maximum(s["mixed"][i], 0.0).astype(BF16)
-    for cp in sems.copies:
-        cp.wait_send()
+    for cp in hidden_copies:
+        cp.wait()
+    sems.sent()
 
 
 def scratch_spec():
@@ -501,6 +518,7 @@
         "lists_out": pltpu.VMEM((8, TILE), jnp.int32),
         "lists_in": pltpu.VMEM((8, TILE), jnp.int32),
         "lists_smem": pltpu.SMEM((8, TILE), jnp.int32),
+        "hidden": pltpu.VMEM((PANELS, TILE, 2 * TILE), BF16),
         "mixed": pltpu.VMEM((PANELS, TILE, 2 * TILE), F32),
         "swap_out": panel(HALVES, 8 * PANELS),
         "swap_in": panel(HALVES, 8 * PANELS),
@@ -533,14 +551,13 @@
 def shards(
     features, tiles, tile_rows, tile_cols, tile_count, panel_lists, self_weight, neigh_weight, bias
 ):
-    vmem = pl.BlockSpec(memory_space=pltpu.VMEM)
     hbm = pl.BlockSpec(memory_space=pltpu.HBM)
     lists = panel_lists[0, 0].T
-    return pl.pallas_call(
+    hidden = pl.pallas_call(
         kernel,
-        out_shape=jax.ShapeDtypeStruct((PANELS * TILE, 2 * TILE), BF16),
+        out_shape=jax.ShapeDtypeStruct((PANELS, TILE, 2 * TILE), BF16),
         in_specs=[hbm] * 9,
-        out_specs=vmem,
+        out_specs=hbm,
         scratch_shapes=list(scratch_spec().values()),
         compiler_params=pltpu.CompilerParams(
             collective_id=0, has_side_effects=True, vmem_limit_bytes=56 << 20
@@ -557,6 +574,7 @@
         neigh_weight,
         bias.reshape(1, 2 * TILE),
     )
+    return hidden.reshape(PANELS * TILE, 2 * TILE)
 
 
 def solution(mesh):

time: 60.3 us -> 60 us (level)
  no operation moved by 1% of the time
where the time goes in v4:
time: 60 us; the launch traced here: 59.9 us
  Pallas kernels  57.5 us (96%)
  local copies, waits for them, and re-layouts  1.67 us (3%)
  between operations  0.66 us (1%)
    pallas_call x1, Pallas kernels, shards(): pl.pallas_call(kernel, out_shape=jax.ShapeDtypeStruct((PANELS, TILE, 2 *...  57.5 us
    unnamed x1, local copies, waits for them, and re-layouts  1.67 us

profile of v4, /device:TPU:24, one launch (start us, length us, event | category | flops | bytes accessed | tf_op | source)
XLA Modules:
  0.0 59.9 jit_solution(10495206702667591976)
XLA Ops:
  0.7 57.5 %sage.1 = bf16[4,128,256]{2,1,0:T(8,128)(2,1)} custom-call(bf16[4,128,256]{2,1,0:T(8,128)(2,1)} %bitcast.11, s32[96,128,128]{2,1,0:T(8,128)} %bitcast.9, s32[1,96]{1,0:T(1,128)} %bitcast.14, s32[1,96]{1,0:T(1,128)} %bitcast.15, s32[1,1]{1,0:T(1,128)S(6)} %copy.11.count_hbm, s32[2,16]{1,0:T(2,128)} %bitcast.12, bf16[256,256]{1,0:T(8,128)(2,1)} %ws_hbm.1, ...), custom_call_target="tpu_custom_call" | custom-call | tf_op jit(solution)/shard_map/sage/pallas_call | solution.py:556
  58.2 1.7 %copy.12 = bf16[512,256]{1,0:T(8,128)(2,1)} copy(bf16[512,256]{1,0:T(8,128)(2,1)} %bitcast.10) | data formatting | bytes 524288

commit v5 on v4

--- a/solution.py
+++ b/solution.py
@@ -328,7 +328,7 @@
             sums[t] = value + sums[s["meta_smem"][0, t]]
             return 0
 
-        lax.fori_loop(lo, hi, body, 0, unroll=24)
+        lax.fori_loop(lo, hi, body, 0, unroll=48)
 
     def owner_col(dy, dx, which):
         hi = x_hi if dx == 0 else 1 - x_hi

time: 60 us -> 59.7 us (level)
  no operation moved by 1% of the time
where the time goes in v5:
time: 59.7 us; the launch traced here: 59.6 us
  Pallas kernels  57.3 us (96%)
  local copies, waits for them, and re-layouts  1.67 us (3%)
  between operations  0.66 us (1%)
    pallas_call x1, Pallas kernels, shards(): pl.pallas_call(kernel, out_shape=jax.ShapeDtypeStruct((PANELS, TILE, 2 *...  57.3 us
    unnamed x1, local copies, waits for them, and re-layouts  1.67 us

profile of v5, /device:TPU:24, one launch (start us, length us, event | category | flops | bytes accessed | tf_op | source)
XLA Modules:
  0.0 59.6 jit_solution(7168845256588316161)
XLA Ops:
  0.7 57.3 %sage.1 = bf16[4,128,256]{2,1,0:T(8,128)(2,1)} custom-call(bf16[4,128,256]{2,1,0:T(8,128)(2,1)} %bitcast.11, s32[96,128,128]{2,1,0:T(8,128)} %bitcast.9, s32[1,96]{1,0:T(1,128)} %bitcast.14, s32[1,96]{1,0:T(1,128)} %bitcast.15, s32[1,1]{1,0:T(1,128)S(6)} %copy.11.count_hbm, s32[2,16]{1,0:T(2,128)} %bitcast.12, bf16[256,256]{1,0:T(8,128)(2,1)} %ws_hbm.1, ...), custom_call_target="tpu_custom_call" | custom-call | tf_op jit(solution)/shard_map/sage/pallas_call | solution.py:556
  57.9 1.7 %copy.12 = bf16[512,256]{1,0:T(8,128)(2,1)} copy(bf16[512,256]{1,0:T(8,128)(2,1)} %bitcast.10) | data formatting | bytes 524288
